TPU v7x, 128 devices: a whole 4x4x4 slice. The times are simulated.
128 devices in a mesh: dp: 32 (over z, y, core), fsdp: 4 (over x).
Axes of the slice: x: 4, y: 4, z: 4, core: 2. Of those that a mesh axis runs over, the one named last changes fastest.
Arguments:
- tokens: bfloat16 [16384, 2048], P(('dp', 'fsdp')), may hold values from -24 to 24
- cotangent: bfloat16 [16384, 2048], P(('dp', 'fsdp')), may hold values from -24 to 24
- block_seq: int32 [32, 4], P('dp'), may hold values from 0 to 1, as said below
- seq_lengths: int32 [32, 2], P('dp'), may hold values from 1 to 384, as said below
- qkv_weight: float32 [2048, 6144], P(('dp', 'fsdp')), may hold values from -0.125 to 0.125
- qkv_moment: float32 [2048, 6144], P(('dp', 'fsdp')), may hold values from -64 to 64
- qkv_second: float32 [2048, 6144], P(('dp', 'fsdp')), may hold values from 4.096 to 65.536
- dense_weight: float32 [2048, 2048], P(('dp', 'fsdp')), may hold values from -0.375 to 0.375
- dense_moment: float32 [2048, 2048], P(('dp', 'fsdp')), may hold values from -16 to 16
- dense_second: float32 [2048, 2048], P(('dp', 'fsdp')), may hold values from 0.32768 to 5.24288
- expand_weight: float32 [2048, 8192], P(('dp', 'fsdp')), may hold values from -0.125 to 0.125
- expand_moment: float32 [2048, 8192], P(('dp', 'fsdp')), may hold values from -24 to 24
- expand_second: float32 [2048, 8192], P(('dp', 'fsdp')), may hold values from 0.73728 to 11.79648
- shrink_weight: float32 [8192, 2048], P(('dp', 'fsdp')), may hold values from -0.0625 to 0.0625
- shrink_moment: float32 [8192, 2048], P(('dp', 'fsdp')), may hold values from -48 to 48
- shrink_second: float32 [8192, 2048], P(('dp', 'fsdp')), may hold values from 2.94912 to 47.5136
- vectors: float32 [22528], P(('dp', 'fsdp')), may hold values from -1 to 1.5
- vec_moment: float32 [22528], P(('dp', 'fsdp')), may hold values from -80 to 80
- vec_second: float32 [22528], P(('dp', 'fsdp')), may hold values from 8.192 to 131.072
Outputs:
- output: bfloat16 [16384, 2048], P(('dp', 'fsdp'))
- input_grad: bfloat16 [16384, 2048], P(('dp', 'fsdp'))
- qkv_grad: float32 [2048, 6144], P(('dp', 'fsdp'))
- qkv_state: float32 [2048, 6144], P(('dp', 'fsdp'))
- qkv_new: float32 [2048, 6144], P(('dp', 'fsdp'))
- dense_grad: float32 [2048, 2048], P(('dp', 'fsdp'))
- dense_state: float32 [2048, 2048], P(('dp', 'fsdp'))
- dense_new: float32 [2048, 2048], P(('dp', 'fsdp'))
- expand_grad: float32 [2048, 8192], P(('dp', 'fsdp'))
- expand_state: float32 [2048, 8192], P(('dp', 'fsdp'))
- expand_new: float32 [2048, 8192], P(('dp', 'fsdp'))
- shrink_grad: float32 [8192, 2048], P(('dp', 'fsdp'))
- shrink_state: float32 [8192, 2048], P(('dp', 'fsdp'))
- shrink_new: float32 [8192, 2048], P(('dp', 'fsdp'))
- vec_grad: float32 [22528], P(('dp', 'fsdp'))
- vec_state: float32 [22528], P(('dp', 'fsdp'))
- vec_new: float32 [22528], P(('dp', 'fsdp'))
Inputs may be any that keep to these rules, and one draw needn't show every extreme that they name: `block_seq`: row g names, for each block of group g in row order, the sequence it holds; every sequence 0 to 1 holds one or more blocks, whose order in the row is the order of its positions; the first and the last block of a row hold the same sequence. `seq_lengths`: A sequence with c blocks has more than 128 * (c - 1) and at most 128 * c tokens; the rest of its last block is padding. In every group one sequence has exactly 128 * (3) tokens.
All inputs are finite; a program needn't handle non-finite values.
Results may differ from a plain program's by a relative error of at most 0.017.
Values may be sent and summed in bfloat16 or wider, within the bound.
A program may use at most 640 MiB of HBM per device.

v0:
```python
import functools

import jax
import jax.numpy as jnp
import numpy as np
from jax import lax
from jax.experimental import pallas as pl
from jax.experimental.pallas import tpu as pltpu
from jax.sharding import Mesh
from jax.sharding import PartitionSpec as P

HEAD = 64
ROT = 32
BLOCK = 128
STEP = 10
GROUP = 512
MODEL = 2048
FF = 8192
PAIR = 2 * HEAD
ALL = ("z", "y", "c", "x")
DP = ("z", "y", "c")
ZY = ("z", "y")
TP = ("c", "x")
SIZES = (4, 4, 2, 4)
TPN = 8
COPIES = 480
SCHEDULE = (
    "s", "vec", "to_d", "to_q", "d", "tok", "to_e", "q", "s", "cot", "vec_rows", "q", "tok",
    "q", "e", "q", "norm_own", "cot", "norm_sides", "q", "norm_far", "e", "d_att", "qkv0", "e",
    "qkv1", "s", "att0", "att1", "s", "e", "att2", "att3", "e", "s", "grad_q0", "grad_q1",
    "sum_q", "grad_d", "up0", "up1", "up2", "sum_q", "up3", "grad_e0", "sum_e0", "sum_q",
    "grad_e1", "downa1", "n1", "downb1", "sum_d", "sum_q", "sum_e1", "downa0", "n1", "downb0",
    "n0", "grad_s0", "back_q", "sum_e0", "sum_d", "n0", "sum_e1", "grad_s1", "outa0", "n1",
    "sum_d", "sum_s1", "sum_s0", "outa1", "col_sums", "sum_e1", "sum_d", "n0", "o1", "outb1",
    "norm_back", "vec_back", "back_d", "o1", "o0", "sum_e0", "outb0", "sum_s1", "o0", "sum_e1",
    "sum_s0", "back_e", "vec_back", "sum_s1", "sum_s0", "o0", "o1", "sum_s1", "sum_s0",
    "vec_back", "sum_s1",
)
SCALE = HEAD ** (-0.5)

NORM_EPS = 1e-05
MASKED = -1e30
BETA_ONE = 0.9
BETA_TWO = 0.999
ADAM_EPS = 1e-08
RATES = (0.02, 0.1, 0.02, 0.01, 0.4)
DECAYS = (0.1, 0.1, 0.1, 0.1, 0.0)
GELU_A = float(np.sqrt(2.0 / np.pi))
GELU_B = 0.044715


def dot(a, b):
    return jnp.dot(a, b, preferred_element_type=jnp.float32)


def dot_t(a, b):
    return lax.dot_general(a, b, (((1,), (1,)), ((), ())), preferred_element_type=jnp.float32)


def cross(a, b):
    return lax.dot_general(a, b, (((0,), (0,)), ((), ())), preferred_element_type=jnp.float32)


def rotary_constants():
    half = np.arange(ROT // 2, dtype=np.float32)
    inverse = (10000.0 ** (-2.0 * half.astype(np.float64) / ROT)).astype(np.float32)
    angle = (np.arange(GROUP, dtype=np.float32)[:, None] * inverse[None, :]).astype(np.float64)
    cosine, sine = np.cos(angle).astype(np.float32), np.sin(angle).astype(np.float32)
    one = np.ones((GROUP, HEAD - ROT), np.float32)
    zero = np.zeros((GROUP, ROT // 2), np.float32)
    rest = np.zeros((GROUP, HEAD - ROT), np.float32)
    turn = np.concatenate([cosine, cosine, one], axis=1)
    ahead = np.concatenate([-sine, zero, rest], axis=1)
    behind = np.concatenate([zero, sine, rest], axis=1)
    return tuple(np.concatenate([a, a], axis=1) for a in (turn, ahead, behind))


MESH = pl.DeviceIdType.MESH


def other(axis, step):
    size = SIZES[ALL.index(axis)]
    return lax.rem(lax.axis_index(axis) + step + size, size)


class Copy:
    def __init__(self, copy):
        self.copy, self.here, self.gone = copy, False, False

    def arrive(self):
        if not self.here:
            self.copy.wait_recv()
        self.here = True

    def leave(self):
        if not self.gone:
            self.copy.wait_send()
        self.gone = True


class Copies:
    def __init__(self, send, recv):
        self.send, self.recv, self.all = send, recv, []

    def start(self, src, dst, to):
        at = len(self.all)
        copy = pltpu.make_async_remote_copy(
            src_ref=src,
            dst_ref=dst,
            send_sem=self.send.at[at],
            recv_sem=self.recv.at[at],
            device_id=to,
            device_id_type=MESH,
        )
        copy.start()
        self.all.append(Copy(copy))
        return self.all[-1]

    def finish(self):
        for copy in self.all:
            copy.leave()


def greet():
    barrier = pltpu.get_barrier_semaphore()
    for partner in token_partners() + weight_partners() + [dense_partner()]:
        pl.semaphore_signal(barrier, inc=1, device_id=partner, device_id_type=MESH)


def enter():
    pl.semaphore_wait(pltpu.get_barrier_semaphore(), 23)


def token_partners():
    return [{"c": other("c", i), "x": other("x", j)} for i in range(2) for j in range(4) if i + j]


def weight_partners():
    return [{"z": other("z", i), "y": other("y", j)} for i in range(4) for j in range(4) if i + j]


def dense_partner():
    z, y, c, x = (lax.axis_index(a) for a in ALL)
    return {"z": (1 - z // 2) * 2 + c, "y": x, "c": lax.rem(z, 2), "x": y}


def gather_weights(copies, view):
    z, y = lax.axis_index("z"), lax.axis_index("y")
    z_up, z_down, y_up, y_down = other("z", 1), other("z", -1), other("y", 1), other("y", -1)
    z_far, y_far = other("z", 2), other("y", 2)
    up, down, far, near = {"y": y_up}, {"y": y_down}, {"z": z_up}, {"z": z_down}

    def go(block, to):
        return copies.start(block, block, to)

    a_up, a_down = go(view(z, y, 4), up), go(view(z, y, 4), down)
    b_up, b_down = go(view(z, y, 5), far), go(view(z, y, 5), near)
    a_own = go(view(z, y, 4), far), go(view(z, y, 4), near)
    b_own = go(view(z, y, 5), up), go(view(z, y, 5), down)
    yield
    a_up.arrive()
    a_low = go(view(z, y_down, 0), up)
    b_up.arrive()
    b_low = go(view(z_down, y, 2), far)
    a_down.arrive()
    a_high = go(view(z, y_up, 1), down)
    b_down.arrive()
    b_high = go(view(z_up, y, 3), near)
    a_side = [(i, go(view(z, i, 4), far), go(view(z, i, 4), near)) for i in (y_down, y_up)]
    b_side = [(i, go(view(i, y, 5), up), go(view(i, y, 5), down)) for i in (z_down, z_up)]
    yield
    last = []
    a_own[0].arrive()
    last.append(go(view(z_down, y, 0), far))
    b_own[0].arrive()
    last.append(go(view(z, y_down, 2), up))
    a_own[1].arrive()
    last.append(go(view(z_up, y, 1), near))
    b_own[1].arrive()
    last.append(go(view(z, y_up, 3), down))
    a_low.arrive()
    a_high.arrive()
    a_side.append((y_far, go(view(z, y_far, 4), far), go(view(z, y_far, 4), near)))
    b_low.arrive()
    b_high.arrive()
    b_side.append((z_far, go(view(z_far, y, 5), up), go(view(z_far, y, 5), down)))
    for k in range(3):
        if k != 1:
            yield
        i, first, second = a_side[k]
        first.arrive()
        last.append(go(view(z_down, i, 0), far))
        second.arrive()
        last.append(go(view(z_up, i, 1), near))
        i, first, second = b_side[k]
        first.arrive()
        last.append(go(view(i, y_down, 2), up))
        second.arrive()
        last.append(go(view(i, y_up, 3), down))
    yield
    for copy in last:
        copy.arrive()


def gather_tokens(copies, ref, sent):
    c, x, across = lax.axis_index("c"), lax.axis_index("x"), other("c", 1)
    right, left = {"x": other("x", 1)}, {"x": other("x", -1)}

    def go(block, to):
        return copies.start(block, block, to)

    own = ref.at[c, x]
    sent.append([go(own, right), go(own, left), go(own, {"c": across})])
    yield
    sent[0][0].arrive()
    last = [go(ref.at[c, other("x", -1), pl.ds(0, 64)], right)]
    side = [go(ref.at[c, other("x", -1)], {"c": across})]
    sent[0][1].arrive()
    last.append(go(ref.at[c, other("x", 1), pl.ds(64, 64)], left))
    side.append(go(ref.at[c, other("x", 1)], {"c": across}))
    sent.append(last + side)
    yield
    for copy in last:
        copy.arrive()
    sent.append([go(ref.at[c, other("x", 2)], {"c": across})])
    yield
    for copies_of_stage in sent:
        for copy in copies_of_stage:
            copy.arrive()
            copy.leave()


def gather_vectors(copies, group, rows, place):
    c, x = lax.axis_index("c"), lax.axis_index("x")
    sent = [copies.start(group.at[c, x], group.at[c, x], to) for to in token_partners()]
    yield
    for copy in sent:
        copy.arrive()
    rows[pl.ds(0, 16), :] = jnp.zeros((16, PAIR), jnp.float32)
    for d in range(TPN):
        rows[pl.ds((176 * d) // PAIR, 3), :] += group[d // 4, d % 4, pl.ds(0, 3), :]
    place[:, pl.ds(0, PAIR)] = rows[pl.ds(0, 16), :].astype(jnp.bfloat16)
    place[:, pl.ds(PAIR, 3 * PAIR)] = jnp.zeros((16, 3 * PAIR), jnp.bfloat16)


def expand_to_group(copies, send, ref, width):
    z, y, c, x = (lax.axis_index(a) for a in ALL)
    rows = pl.ds(pl.multiple_of((c * 4 + x) * 16, 16), 16)
    sent = []
    for to in token_partners():
        sent.append(copies.start(send.at[to["c"] * 4 + to["x"]], ref.at[z, y, rows], to))
    ref[z, y, rows] = send[c * 4 + x]
    yield
    for copy in sent:
        copy.arrive()


def by_rows(ref, rows):
    quarter = rows // 4

    def view(z, y, part):
        start, size = (part * quarter, quarter) if part < 4 else ((part - 4) * 2 * quarter, 2 * quarter)
        return ref.at[z, y, pl.ds(start, size)]

    return view


def by_columns(ref, columns):
    quarter = columns // 4

    def view(z, y, part):
        start, size = (part * quarter, quarter) if part < 4 else ((part - 4) * 2 * quarter, 2 * quarter)
        return ref.at[z, y, :, pl.ds(start, size)]

    return view


def step(*works):
    for work in works:
        next(work, None)


def row_of(ref, first, count):
    return jnp.concatenate([ref[pl.ds(first + i, 1), :] for i in range(count)], axis=1)


def ring_sum(copies, axis, block, land, low_part, high_part):
    ahead, behind = other(axis, 1), other(axis, -1)
    up, down = {axis: ahead}, {axis: behind}
    far = other(axis, 2)
    t_low = copies.start(block(far, low_part), land.at[0], up)
    t_high = copies.start(block(far, high_part), land.at[1], down)
    d_high = copies.start(block(ahead, high_part), land.at[3], up)
    d_low = copies.start(block(behind, low_part), land.at[2], down)
    yield
    t_low.arrive()
    land[0] = land[0] + block(ahead, low_part)[...]
    p_low = copies.start(land.at[0], land.at[4], up)
    t_high.arrive()
    land[1] = land[1] + block(behind, high_part)[...]
    p_high = copies.start(land.at[1], land.at[5], down)
    yield
    for copy in (d_low, d_high, p_low, p_high):
        copy.arrive()
    for copy in (t_low, t_high, d_low, d_high, p_low, p_high):
        copy.leave()


def three(own, land, high, at=...):
    f32 = jnp.float32
    first, second = land.at[4 + high], land.at[2 + high]
    return own[at].astype(f32) + first[at].astype(f32) + second[at].astype(f32)


def both(first, second):
    while True:
        done = [next(first, 0), next(second, 0)]
        if 0 in done:
            return
        yield


def scatter_weights(copies, view, wide, narrow, give):
    z, y = lax.axis_index("z"), lax.axis_index("y")
    every = slice(None)
    low = jnp.bfloat16
    yield from both(
        ring_sum(copies, "y", lambda i, p: view(every, i, p), wide.at[0], 0, 1),
        ring_sum(copies, "z", lambda i, p: view(i, every, p), wide.at[1], 2, 3),
    )
    for high in range(2):
        own = view(every, y, high)
        for i in range(4):
            own[i] = three(own, wide.at[0], high, i).astype(low)
        own = view(z, every, 2 + high)
        for i in range(4):
            own[i] = three(own, wide.at[1], high, i).astype(low)
    yield from both(
        ring_sum(copies, "z", lambda i, p: view(i, y, p), narrow.at[0], 0, 1),
        ring_sum(copies, "y", lambda i, p: view(z, i, p), narrow.at[1], 2, 3),
    )
    for high in range(2):
        give(high, three(view(z, y, high), narrow.at[0], high))
        give(2 + high, three(view(z, y, 2 + high), narrow.at[1], high))


def scatter_tokens(copies, ref, core_land, land, give, core_free, ring_free, first):
    c, x, across = lax.axis_index("c"), lax.axis_index("x"), other("c", 1)
    if not first:
        pl.semaphore_wait(core_free, 1)
    came = copies.start(ref.at[across], core_land, {"c": across})
    yield
    came.arrive()
    for i in range(4):
        ref[c, i] = ref[c, i] + core_land[i]
    if first:
        pl.semaphore_signal(core_free, inc=1, device_id={"c": across}, device_id_type=MESH)
    else:
        pl.semaphore_wait(ring_free, 2)
    yield from ring_sum(copies, "x", lambda i, p: ref.at[c, i, pl.ds(p * 64, 64)], land, 0, 1)
    for high in range(2):
        own = ref.at[c, x, pl.ds(high * 64, 64)]

        def chunk(r, _):
            rows = pl.ds(pl.multiple_of(r * 16, 16), 16)
            give(high, r, three(own, land, high, rows))
            return 0

        lax.fori_loop(0, 4, chunk, 0)
    if first:
        for way in (1, -1):
            to = {"x": other("x", way)}
            pl.semaphore_signal(ring_free, inc=1, device_id=to, device_id_type=MESH)


def landed(copy):
    yield
    copy.arrive()


def sum_vectors(copies, part, came, mine, zy, out):
    z, y, c, x = (lax.axis_index(a) for a in ALL)
    t = c * 4 + x
    sent = [
        copies.start(part.at[to["c"] * 4 + to["x"]], came.at[t], to) for to in token_partners()
    ]
    came[t] = part[t]
    yield
    for copy in sent:
        copy.arrive()
    total = jnp.sum(came[...], axis=0)
    for i in range(6):
        mine[pl.ds(i, 1), :] = total[i // 2 : i // 2 + 1, (i % 2) * PAIR : (i % 2 + 1) * PAIR]
    zy[z, y] = mine[...]
    sent = [copies.start(mine, zy.at[z, y], to) for to in weight_partners()]
    yield
    for copy in sent:
        copy.arrive()
    out[c, x] = jnp.sum(zy[...].reshape(16, 24, PAIR), axis=0)
    sent = [copies.start(out.at[c, x], out.at[c, x], to) for to in token_partners()]
    yield
    for copy in sent:
        copy.arrive()


def return_to_group(copies, ref, out):
    c, x = lax.axis_index("c"), lax.axis_index("x")
    t = c * 4 + x
    sent = []
    for to in token_partners():
        sent.append(copies.start(ref.at[to["c"] * 4 + to["x"]], out.at[t], to))
    out[t] = ref[t]
    yield
    for copy in sent:
        copy.arrive()


def turned(values, table, sign):
    turn, ahead, behind = table
    up = pltpu.roll(values, PAIR - ROT // 2, 1)
    down = pltpu.roll(values, ROT // 2, 1)
    if sign > 0:
        return values * turn + up * ahead + down * behind
    return values * turn - up * ahead - down * behind


def attend(meta, turn_ref, qkv, att, g, p):
    low, f32 = jnp.bfloat16, jnp.float32
    lane = lax.broadcasted_iota(jnp.int32, (BLOCK, PAIR), 1)
    first = lane < HEAD
    zero = jnp.zeros((BLOCK, PAIR), low)
    row_at = lax.broadcasted_iota(jnp.int32, (BLOCK, BLOCK), 0)
    col_at = lax.broadcasted_iota(jnp.int32, (BLOCK, BLOCK), 1)
    cols = [pl.ds(pl.multiple_of(i * 2 * PAIR + p * PAIR, PAIR), PAIR) for i in range(3)]
    d_k = [jnp.zeros((BLOCK, PAIR), f32) for _ in range(4)]
    d_v = [jnp.zeros((BLOCK, PAIR), f32) for _ in range(4)]
    held = [qkv[g, :, cols[i]] for i in range(3)] + [att[g, :, cols[0]]]
    done = []
    for b in range(4):
        rows, width = slice(b * BLOCK, (b + 1) * BLOCK), (b + 1) * BLOCK
        base = meta[:, 4 + b : 5 + b] * BLOCK
        diagonal = (col_at <= row_at) & (col_at.astype(f32) + base < meta[:, 8 + b : 9 + b])
        bias = [
            jnp.where(meta[:, e : e + 1] == meta[:, b : b + 1], 0.0, MASKED)
            + jnp.zeros((BLOCK, BLOCK), f32)
            for e in range(b)
        ]
        bias.append(jnp.where(diagonal, 0.0, MASKED).astype(f32))
        bias = bias[0] if b == 0 else jnp.concatenate(bias, axis=1)
        q, da, k, v = held[0][rows], held[3][rows], held[1][:width], held[2][:width]
        qs = jnp.concatenate([jnp.where(first, q, zero), jnp.where(first, zero, q)], axis=0)
        das = jnp.concatenate([jnp.where(first, da, zero), jnp.where(first, zero, da)], axis=0)
        scores = dot_t(qs, k) + jnp.concatenate([bias, bias], axis=0)
        w = jnp.exp(scores - jnp.max(scores, axis=1, keepdims=True))
        prob = w * (1.0 / jnp.sum(w, axis=1, keepdims=True))
        prob_low = prob.astype(low)
        summed = dot(prob_low, v)
        dp = dot_t(das, v)
        ds = (prob * (dp - jnp.sum(prob * dp, axis=1, keepdims=True))).astype(low)
        dq = dot(ds, k)
        dq = jnp.where(first, dq[:BLOCK], dq[BLOCK:]) * SCALE
        dq = turned(dq, table_of(meta, turn_ref, b), -1).astype(low)
        done.append((jnp.where(first, summed[:BLOCK], summed[BLOCK:]).astype(low), dq))
        dk = cross(ds, qs)
        dv = cross(prob_low, das)
        for e in range(b + 1):
            d_k[e] = d_k[e] + dk[e * BLOCK : (e + 1) * BLOCK]
            d_v[e] = d_v[e] + dv[e * BLOCK : (e + 1) * BLOCK]
    for b in range(4):
        rows = pl.ds(b * BLOCK, BLOCK)
        att[g, rows, cols[0]], qkv[g, rows, cols[0]] = done[b]
        qkv[g, rows, cols[1]] = turned(d_k[b], table_of(meta, turn_ref, b), -1).astype(low)
        qkv[g, rows, cols[2]] = d_v[b].astype(low)


def table_of(meta, turn_ref, b):
    rank = meta[:, 4 + b : 5 + b]
    parts = [turn_ref[:, pl.ds(r * BLOCK, BLOCK), :] for r in range(3)]
    table = jnp.where((rank == 0.0)[None], parts[0], jnp.where((rank == 1.0)[None], parts[1], parts[2]))
    return table[0], table[1], table[2]


def layer_kernel(
    tokens_ref, cot_ref, seq_ref, length_ref, vec_ref, turn_ref, q_hbm, d_hbm, e_hbm, s_hbm,
    out_ref, ig_ref, ge_out, gq_out, gd_out, gs_out, vec_out,
    we, wq, wd, ws, normed, d_out, act, d_pre, qkv, att,
    ge, gq, gd, gs, stage, bias_e, vec_group, vec_rows, we_send, wq_send, wd_own,
    wide_e, narrow_e, wide_d, narrow_d, wide_s, narrow_s,
    core_land, ring_land, res_e, res_q, res_d,
    vec_line, vec_sum, vec_part, vec_came, vec_mine, vec_zy,
    send, recv, local, core_free, ring_free, wide_free,
):
    low, f32 = jnp.bfloat16, jnp.float32
    z, y, c, x = (lax.axis_index(a) for a in ALL)
    t = c * 4 + x
    copies = Copies(send, recv)
    greet()

    loads = [
        pltpu.make_async_copy(q_hbm, stage.at[pl.ds(16, 16), pl.ds(0, 6144)], local.at[0]),
        pltpu.make_async_copy(d_hbm, stage.at[pl.ds(16, 16), pl.ds(6144, 2048)], local.at[1]),
        pltpu.make_async_copy(e_hbm, stage.at[pl.ds(0, 16)], local.at[2]),
    ]
    for k in range(4):
        rows = pl.ds(16 * k, 16)
        place = stage.at[pl.ds(32, 16), pl.ds(2048 * k, 2048)]
        loads.append(pltpu.make_async_copy(s_hbm.at[rows], place, local.at[3 + k]))
    for load in loads:
        load.start()

    lane = lax.broadcasted_iota(jnp.int32, (1, PAIR), 1)
    seqs = [seq_ref[0, b] for b in range(4)]
    own_meta = jnp.zeros((1, PAIR), f32)
    own_rank, own_limit = jnp.zeros((1, 1), f32), jnp.zeros((1, 1), f32)
    for b in range(4):
        rank = jnp.int32(0)
        for e in range(b):
            rank = rank + jnp.where(seqs[e] == seqs[b], 1, 0)
        limit = jnp.where(seqs[b] == 0, length_ref[0, 0], length_ref[0, 1])
        for at, value in ((b, seqs[b]), (4 + b, rank), (8 + b, limit)):
            own_meta = jnp.where(lane == at, value.astype(f32), own_meta)
        own_rank = jnp.where(x == b, rank.astype(f32), own_rank)
        own_limit = jnp.where(x == b, limit.astype(f32), own_limit)
    vec_line[...] = jnp.zeros_like(vec_line)
    vec_line[pl.ds(0, 1), pl.ds(0, 176)] = vec_ref[...].astype(low).astype(f32)
    line = pltpu.roll(vec_line[...], 16 * lax.rem(3 * t + 24 * (z * 4 + y), 8), 1)
    vec_own = vec_group.at[c, x]
    vec_own[...] = jnp.zeros((8, PAIR), f32)
    for k in range(3):
        vec_own[pl.ds(k, 1), :] = line[0:1, k * PAIR : (k + 1) * PAIR]
    vec_own[pl.ds(4, 1), :] = own_meta

    def d_out_rows(rows, first):
        row_at = lax.broadcasted_iota(jnp.int32, (16, 1), 0) + first
        live = (row_at.astype(f32) + own_rank * BLOCK < own_limit).astype(f32)
        return cot_ref[rows, :].astype(f32) * live

    def mask_chunk(r, _):
        rows = pl.ds(pl.multiple_of(r * 16, 16), 16)
        d_out[c, x, rows] = d_out_rows(rows, r * 16).astype(low)
        return 0


    def scaled(rows):
        values = tokens_ref[rows, :].astype(f32)
        middle = values - jnp.mean(values, axis=1, keepdims=True)
        spread = lax.rsqrt(jnp.mean(middle * middle, axis=1, keepdims=True) + NORM_EPS)
        return middle * spread, spread

    def scale_chunk(r, _):
        rows = pl.ds(pl.multiple_of(r * 16, 16), 16)
        normed[c, x, rows] = scaled(rows)[0].astype(low)
        return 0

    lax.fori_loop(0, 8, scale_chunk, 0)
    loads[0].wait()
    for k in range(8):
        for i in range(6):
            col = (i // 2) * 2048 + (1 - i % 2) * 1024 + k * PAIR
            piece = stage[pl.ds(16, 16), pl.ds(col, PAIR)]
            wq_send[k, :, pl.ds(i * PAIR, PAIR)] = piece.astype(low)
    enter()

    def cast_dense():
        loads[1].wait()
        wd_own[...] = stage[pl.ds(16, 16), pl.ds(6144, 2048)].astype(low)

    def cast_expand():
        left16 = lax.broadcasted_iota(jnp.int32, (16, PAIR), 1) < HEAD
        loads[2].wait()
        for j in range(8):
            for k in range(4):
                first = stage[pl.ds(0, 16), pl.ds(j * 1024 + k * PAIR, PAIR)]
                second = stage[pl.ds(0, 16), pl.ds(j * 1024 + 512 + k * PAIR, PAIR)]
                even = jnp.where(left16, first, pltpu.roll(second, HEAD, 1))
                odd = jnp.where(left16, pltpu.roll(first, HEAD, 1), second)
                we_send[2 * k, :, pl.ds(j * PAIR, PAIR)] = even.astype(low)
                we_send[2 * k + 1, :, pl.ds(j * PAIR, PAIR)] = odd.astype(low)

    def cast_shrink():
        for k in range(4):
            loads[3 + k].wait()
            ws[z, y, pl.ds(16 * k, 16)] = stage[pl.ds(32, 16), pl.ds(2048 * k, 2048)].astype(low)

    works, stages, tasks, finished = {}, {}, {}, set()
    token_sends = []

    def finish(*names):
        for name in names:
            for _ in works[name]:
                pass
            finished.add(name)

    def advance(name):
        if name not in works:
            works[name], stages[name] = begin(name), 0
        stages[name] += 1
        if next(works[name], 0) == 0:
            finished.add(name)

    def reach(name, stage):
        while stages[name] < stage:
            advance(name)

    def begin(name):
        if name == "vec":
            return gather_vectors(copies, vec_group, vec_rows, wd.at[z, y, :, pl.ds(MODEL, 512)])
        if name == "to_q":
            return expand_to_group(copies, wq_send, wq, 768)
        if name == "to_e":
            cast_expand()
            return expand_to_group(copies, we_send, we, 1024)
        if name == "to_d":
            cast_dense()
            there = dense_partner()
            place = wd.at[there["z"], there["y"], :, pl.ds(0, MODEL)]
            return landed(copies.start(wd_own, place, there))
        if name == "q":
            finish("to_q")
            return gather_weights(copies, by_rows(wq, 128))
        if name == "d":
            finish("to_d", "vec")
            return gather_weights(copies, by_columns(wd, 2560))
        if name == "e":
            finish("to_e")
            return gather_weights(copies, by_rows(we, 128))
        if name == "s":
            cast_shrink()
            return gather_weights(copies, by_rows(ws, 64))
        if name == "cot":
            lax.fori_loop(0, 8, mask_chunk, 0)
            return gather_tokens(copies, d_out, [])
        if name == "tok":
            return gather_tokens(copies, normed, token_sends)
        if name == "sum_d":
            return scatter_weights(copies, by_columns(gd, 2048), wide_d, narrow_d, give_d)
        if name == "sum_q":
            return sum_q()
        if name in ("sum_e0", "sum_e1"):
            half = int(name[-1])
            cols = pl.ds(half * 512, 512)
            return scatter_weights(
                copies,
                by_rows(ge.at[:, :, :, cols], 128),
                wide_e.at[:, :, :, :, cols],
                narrow_e.at[:, :, :, cols],
                give_e(half),
            )
        if name in ("sum_s0", "sum_s1"):
            finish("sum_q")
            if "wide" not in finished:
                pl.semaphore_wait(wide_free, 4)
                finished.add("wide")
            half = int(name[-1])
            cols = pl.ds(half * 1024, 1024)
            return scatter_weights(
                copies,
                by_rows(gs.at[:, :, :, cols], 64),
                wide_s.at[:, :, :, :, cols],
                narrow_s.at[:, :, :, cols],
                give_s(half),
            )
        if name in ("n0", "n1", "o0", "o1"):
            half = int(name[-1])
            if name[0] == "o":
                finish("n" + name[1])
            cols = pl.ds(half * 1024, 1024)
            return scatter_tokens(
                copies,
                (normed if name[0] == "n" else d_out).at[:, :, :, cols],
                core_land.at[:, :, cols],
                ring_land.at[:, :, cols],
                (give_n if name[0] == "n" else give_o)(half),
                core_free.at[half],
                ring_free.at[half],
                name[0] == "n",
            )
        if name == "back_q":
            finish("sum_q")
            return return_to_group(copies, res_q, gq_out)
        if name == "back_e":
            finish("sum_e0", "sum_e1")
            return return_to_group(copies, res_e, ge_out)
        if name == "back_d":
            finish("sum_d")
            return landed(copies.start(res_d, gd_out, dense_partner()))
        return sum_vectors(copies, vec_part, vec_came, vec_mine, vec_zy, vec_out)

    def vec_task():
        finish("d")
        for i in range(16):
            block = wd[i // 4, i % 4, :, pl.ds(MODEL, PAIR)].astype(f32)
            vec_rows[pl.ds(11 * i, 11), :] = block[0:11]

    def norm_blocks(blocks):
        def chunk(r, _):
            rows = pl.ds(pl.multiple_of(r * 16, 16), 16)
            for core, chip in blocks:
                xhat = normed[core, chip, rows].astype(f32)
                whole = xhat * row_of(vec_rows, 0, 16) + row_of(vec_rows, 16, 16)
                normed[core, chip, rows] = whole.astype(low)
            return 0

        lax.fori_loop(0, 8, chunk, 0)

    def norm_own():
        reach("tok", 2)
        for copy in token_sends[0]:
            copy.leave()
        token_sends[0][2].arrive()
        norm_blocks([(c, x), (1 - c, x)])

    def norm_sides():
        reach("tok", 3)
        for copy in token_sends[1]:
            copy.leave()
        for copy in token_sends[1][2:]:
            copy.arrive()
        for way in (-1, 1):
            norm_blocks([(c, other("x", way)), (1 - c, other("x", way))])

    def norm_far():
        finish("tok")
        token_sends[2][0].leave()
        norm_blocks([(c, other("x", 2)), (1 - c, other("x", 2))])

    def qkv_tile(g, _):
        meta = vec_group[g, x, pl.ds(4, 1), :]
        projected = dot(normed[g].reshape(512, MODEL), wq[...].reshape(MODEL, 768))
        for p in range(6):
            bias = vec_rows[pl.ds(32 + (p // 2) * 16 + (1 - p % 2) * 8 + t, 1), :]
            for b in range(4):
                rows = pl.ds(b * BLOCK, BLOCK)
                part = projected[b * BLOCK : (b + 1) * BLOCK, p * PAIR : (p + 1) * PAIR] + bias
                if p < 4:
                    part = turned(part, table_of(meta, turn_ref, b), 1)
                part = part.astype(low)
                if p < 2:
                    part = part * jnp.asarray(SCALE, low)
                qkv[g, rows, pl.ds(p * PAIR, PAIR)] = part
        return 0

    def d_att_tile(g, _):
        dense = wd[:, :, :, pl.ds(0, MODEL)].reshape(256, MODEL)
        att[g] = dot_t(d_out[g].reshape(512, MODEL), dense).astype(low)
        return 0

    def d_att_task():
        finish("cot", "d")
        lax.fori_loop(0, 2, d_att_tile, 0)

    def qkv_task(g):
        def task():
            finish("tok", "q")
            lax.fori_loop(g, g + 1, qkv_tile, 0)

        return task

    def attend_tile(i, _):
        g, p = i // 2, lax.rem(i, 2)
        attend(vec_group[g, x, pl.ds(4, 1), :], turn_ref, qkv, att, g, p)
        return 0

    def dense_tile(n, _):
        cols = pl.ds(pl.multiple_of(n * 1024, 1024), 1024)
        term = cross(att[...].reshape(1024, 256), d_out[:, :, :, cols].reshape(1024, 1024))
        gd[:, :, :, cols] = term.astype(low).reshape(4, 4, 16, 1024)
        return 0

    def give_d(part, total):
        res_d[:, pl.ds(part * 512, 512)] = total.astype(low)

    def qkv_grad_tile(i, _):
        mine = normed[:, :, :, pl.ds(pl.multiple_of(i * 512, 512), 512)].reshape(1024, 512)
        term = cross(mine, qkv[...].reshape(1024, 768)).astype(low).reshape(4, BLOCK, 768)
        gq[i, :, :, pl.ds(0, 768)] = term[:, :64]
        gq[i, :, :, pl.ds(768, 768)] = term[:, 64:]
        return 0

    def give_q(part, total):
        res_q[part] = total[:, :768].astype(low)
        res_q[4 + part] = total[:, 768:].astype(low)

    def sum_q():
        short = pl.ds(0, 1536)
        yield from scatter_weights(
            copies,
            by_rows(gq, 64),
            wide_s.at[:, :, :, :, short],
            narrow_s.at[:, :, :, short],
            give_q,
        )
        for axis in ("y", "z"):
            for way in (1, -1):
                to = {axis: other(axis, way)}
                pl.semaphore_signal(wide_free, inc=1, device_id=to, device_id_type=MESH)

    def up_tile(i, _):
        g, n = i // 2, lax.rem(i, 2)
        cols = pl.ds(pl.multiple_of(n * 512, 512), 512)
        pre_term = dot(normed[g].reshape(512, MODEL), we[:, :, :, cols].reshape(MODEL, 512))
        for k in range(8):
            stage[:, pl.ds(k * 512, 512)] = pre_term[k * 64 : k * 64 + 64]
        act_term = dot_t(d_out[g].reshape(512, MODEL), ws[pl.ds(2 * n, 2)].reshape(512, MODEL))
        for k in range(8):
            stage[:, pl.ds(4096 + k * 512, 512)] = act_term[k * 64 : k * 64 + 64]

        def chunk(r, _):
            rows = pl.ds(pl.multiple_of(r * 16, 16), 16)
            at = pl.ds(pl.multiple_of(lax.rem(r, 4) * 16, 16), 16)
            across = r // 4
            pre = stage[at, pl.ds(pl.multiple_of(across * 512, 512), 512)]
            pre = pre + bias_e[pl.ds(0, 1), cols]
            square = pre * pre
            inner = jnp.tanh(GELU_A * (pre + GELU_B * (square * pre)))
            cover = 0.5 + 0.5 * inner
            act[g, rows, cols] = (pre * cover).astype(low)
            slope = cover + 0.5 * pre * (1.0 - inner * inner) * (
                GELU_A + (3.0 * GELU_A * GELU_B) * square
            )
            d_act = stage[at, pl.ds(pl.multiple_of(4096 + across * 512, 512), 512)]
            d_pre[g, rows, cols] = (d_act * slope).astype(low)
            return 0

        lax.fori_loop(0, 32, chunk, 0, unroll=4)
        return 0

    def up_bias():
        odd = lax.rem(t, 2) == 1
        half = t // 2
        left = lane < HEAD
        bias_e[...] = jnp.zeros_like(bias_e)
        for j in range(8):
            r0 = vec_rows[pl.ds(96 + 8 * j + half, 1), :]
            r1 = vec_rows[pl.ds(100 + 8 * j + half, 1), :]
            even_row = jnp.where(left, r0, pltpu.roll(r1, HEAD, 1))
            odd_row = jnp.where(left, pltpu.roll(r0, HEAD, 1), r1)
            bias_e[pl.ds(0, 1), pl.ds(j * PAIR, PAIR)] = jnp.where(odd, odd_row, even_row)

    def up_task(i):
        def task():
            finish("e", "s")
            if i == 0:
                up_bias()
            lax.fori_loop(i, i + 1, up_tile, 0)

        return task

    def expand_tile(half):
        cols = pl.ds(half * 512, 512)

        def body(i, _):
            mine = normed[:, :, :, pl.ds(pl.multiple_of(i * 1024, 1024), 1024)].reshape(1024, 1024)
            term = cross(mine, d_pre[:, :, cols].reshape(1024, 512))
            ge[pl.ds(2 * i, 2), :, :, cols] = term.astype(low).reshape(2, 4, BLOCK, 512)
            return 0

        return body

    def give_e(half):
        def give(part, total):
            cols = pl.ds(half * 512, 512)
            res_e[pl.ds(2 * part, 2), :, cols] = total.astype(low).reshape(2, 16, 512)

        return give

    def shrink_tile(half):
        cols = pl.ds(half * 1024, 1024)

        def body(j, _):
            mine = act[:, :, pl.ds(pl.multiple_of(j * 512, 512), 512)].reshape(1024, 512)
            term = cross(mine, d_out[:, :, :, cols].reshape(1024, 1024))
            gs[pl.ds(2 * j, 2), :, :, cols] = term.astype(low).reshape(2, 4, 64, 1024)
            return 0

        return body

    def give_s(half):
        def give(part, total):
            gs_out[pl.ds(part * 16, 16), pl.ds(half * 1024, 1024)] = total

        return give

    def down_task(g, half):
        def task():
            term = dot_t(qkv[g], wq[2 * half : 2 * half + 2].reshape(1024, 768)) + dot_t(
                d_pre[g], we[2 * half : 2 * half + 2].reshape(1024, 1024)
            )
            cols = pl.ds(half * 1024, 1024)
            normed[g, :, :, cols] = term.astype(low).reshape(4, BLOCK, 1024)

        return task

    def give_n(half):
        def give(high, r, total):
            at = pl.ds(pl.multiple_of(r * 16, 16), 16)
            stage[at, pl.ds(high * 2048 + half * 1024, 1024)] = total

        return give

    def out_task(g, half):
        def task():
            cols = pl.ds(half * 1024, 1024)
            term = dot(att[g], wd[:, :, :, cols].reshape(256, 1024)) + dot(
                act[g], ws[:, :, :, cols].reshape(1024, 1024)
            )
            d_out[g, :, :, cols] = term.astype(low).reshape(4, BLOCK, 1024)

        return task

    def give_o(half):
        def give(high, r, total):
            rows = pl.ds(pl.multiple_of(high * 64 + r * 16, 16), 16)
            cols = pl.ds(half * 1024, 1024)
            add_bias = row_of(vec_rows, 80 + half * 8, 8) + row_of(vec_rows, 160 + half * 8, 8)
            out_ref[rows, cols] = (tokens_ref[rows, cols].astype(f32) + (total + add_bias)).astype(low)

        return give

    def norm_back():
        finish("n0", "n1")
        gain = row_of(vec_rows, 0, 16)
        vec_sum[...] = jnp.zeros_like(vec_sum)

        def chunk(r, _):
            rows = pl.ds(pl.multiple_of(r * 16, 16), 16)
            at = pl.ds(pl.multiple_of(lax.rem(r, 4) * 16, 16), 16)
            total = stage[at, pl.ds(pl.multiple_of((r // 4) * 2048, 2048), 2048)]
            xhat, spread = scaled(rows)
            e = total * gain
            mean_e = jnp.mean(e, axis=1, keepdims=True)
            mean_x = jnp.mean(e * xhat, axis=1, keepdims=True)
            dy = d_out_rows(rows, r * 16)
            ig_ref[rows, :] = (dy + spread * (e - mean_e - xhat * mean_x)).astype(low)
            for i, value in enumerate((total * xhat, total, dy)):
                vec_sum[i] += value[0:8] + value[8:16]
            return 0

        lax.fori_loop(0, 8, chunk, 0)
        vec_part[...] = jnp.zeros_like(vec_part)
        for i in range(3):
            total = jnp.sum(vec_sum[i], axis=0, keepdims=True)
            for k in range(8):
                vec_part[k, pl.ds(i, 1), :] = total[:, k * 256 : k * 256 + 256]

    def column_sums():
        ones = jnp.ones((8, 1024), low)
        vec_mine[...] = jnp.zeros_like(vec_mine)
        qkv_sum = dot(ones, qkv[...].reshape(1024, 768))
        for i in range(6):
            vec_mine[pl.ds(6 + i, 1), :] = qkv_sum[0:1, i * PAIR : (i + 1) * PAIR]
        pre_sum = dot(ones, d_pre[...].reshape(1024, 1024))
        for i in range(8):
            vec_mine[pl.ds(12 + i, 1), :] = pre_sum[0:1, i * PAIR : (i + 1) * PAIR]

    def loop(first, last, tile):
        return lambda: lax.fori_loop(first, last, tile, 0)

    tasks = {
        "vec_rows": vec_task, "norm_own": norm_own, "norm_sides": norm_sides, "norm_far": norm_far,
        "d_att": d_att_task, "qkv0": qkv_task(0), "qkv1": qkv_task(1), "grad_d": loop(0, 2, dense_tile),
        "grad_q0": loop(0, 2, qkv_grad_tile), "grad_q1": loop(2, 4, qkv_grad_tile),
        "grad_e0": loop(0, 2, expand_tile(0)), "grad_e1": loop(0, 2, expand_tile(1)),
        "grad_s0": loop(0, 2, shrink_tile(0)), "grad_s1": loop(0, 2, shrink_tile(1)),
        "norm_back": norm_back, "col_sums": column_sums,
    }
    for i in range(4):
        tasks["att" + str(i)] = loop(i, i + 1, attend_tile)
        tasks["up" + str(i)] = up_task(i)
    for half in range(2):
        for at, g in (("a", 1 - c), ("b", c)):
            tasks["down" + at + str(half)] = down_task(g, half)
            tasks["out" + at + str(half)] = out_task(g, half)

    for name in SCHEDULE:
        if name in tasks:
            tasks[name]()
        else:
            advance(name)
    finish(*works)
    copies.finish()


def layer(tokens, cotangent, block_seq, seq_lengths, vectors, weights):
    low, f32 = jnp.bfloat16, jnp.float32
    vmem = pl.BlockSpec(memory_space=pltpu.VMEM)
    smem = pl.BlockSpec(memory_space=pltpu.SMEM)
    anywhere = pl.BlockSpec(memory_space=pl.ANY)
    turn = jnp.asarray(np.stack(rotary_constants())[:, : 3 * BLOCK])
    outs = [
        ((BLOCK, MODEL), low), ((BLOCK, MODEL), low), ((8, 16, 1024), low), ((8, 16, 768), low),
        ((16, MODEL), low), ((64, MODEL), f32), ((2, 4, 24, PAIR), f32),
    ]
    held = [
        ((4, 4, 128, 1024), low), ((4, 4, 128, 768), low), ((4, 4, 16, 2560), low),
        ((4, 4, 64, 2048), low), ((2, 4, 128, 2048), low), ((2, 4, 128, 2048), low),
        ((2, 512, 1024), low), ((2, 512, 1024), low), ((2, 512, 768), low), ((2, 512, 256), low),
        ((4, 4, 128, 1024), low), ((4, 4, 64, 1536), low), ((4, 4, 16, 2048), low),
        ((4, 4, 64, 2048), low), ((64, 8192), f32), ((8, 1024), f32),
        ((2, 4, 8, 128), f32), ((184, 128), f32),
        ((8, 16, 1024), low), ((8, 16, 768), low), ((16, 2048), low),
        ((2, 6, 4, 32, 1024), low), ((2, 6, 32, 1024), low),
        ((2, 6, 4, 16, 512), low), ((2, 6, 16, 512), low),
        ((2, 6, 4, 16, 2048), low), ((2, 6, 16, 2048), low),
        ((4, 128, 2048), low), ((6, 64, 2048), low),
        ((8, 16, 1024), low), ((8, 16, 768), low), ((16, 2048), low), ((8, 384), f32),
        ((3, 8, MODEL), f32), ((8, 8, 256), f32), ((8, 8, 256), f32), ((24, 128), f32),
        ((4, 4, 24, 128), f32),
    ]
    return pl.pallas_call(
        layer_kernel,
        in_specs=[vmem, vmem, smem, smem, vmem, vmem] + [anywhere] * 4,
        out_specs=[vmem] * 7,
        out_shape=[jax.ShapeDtypeStruct(s, k) for s, k in outs],
        scratch_shapes=[pltpu.VMEM(s, k) for s, k in held]
        + [
            pltpu.SemaphoreType.DMA((COPIES,)),
            pltpu.SemaphoreType.DMA((COPIES,)),
            pltpu.SemaphoreType.DMA((7,)),
            pltpu.SemaphoreType.REGULAR((2,)),
            pltpu.SemaphoreType.REGULAR((2,)),
            pltpu.SemaphoreType.REGULAR,
        ],
        compiler_params=pltpu.CompilerParams(
            collective_id=0, has_side_effects=True, vmem_limit_bytes=64 * 2**20
        ),
        name="layer",
    )(tokens, cotangent, block_seq, seq_lengths, vectors[None, :], turn, *weights)


def update_kernel(out_in, ig_in, ge, gq, gd, gs, vec, *refs):
    f32 = jnp.float32
    masters, moments, seconds = refs[0:5], refs[5:10], refs[10:15]
    out_ref, ig_ref = refs[15:17]
    results = [refs[17 + 3 * i : 20 + 3 * i] for i in range(5)]
    flat = refs[32]
    out_ref[...] = out_in[...]
    ig_ref[...] = ig_in[...]

    def update(i, at, gradient):
        grad_ref, state_ref, new_ref = results[i]
        grad_ref[at] = gradient
        state, new = adam_step(
            masters[i][at], moments[i][at], seconds[i][at], gradient, RATES[i], DECAYS[i]
        )
        state_ref[at] = state
        new_ref[at] = new

    every = slice(None)
    for s in range(3):
        for hi in range(2):
            for t in range(TPN):
                col = s * MODEL + hi * 1024 + t * PAIR
                piece = gq[t, :, pl.ds((2 * s + 1 - hi) * PAIR, PAIR)].astype(f32)
                update(0, (every, pl.ds(col, PAIR)), piece)
    for k in range(16):
        cols = (every, pl.ds(k * PAIR, PAIR))
        update(1, cols, gd[cols].astype(f32))
        for r in range(4):
            at = (pl.ds(16 * r, 16), pl.ds(k * PAIR, PAIR))
            update(3, at, gs[at])
    left = lax.broadcasted_iota(jnp.int32, (16, PAIR), 1) < HEAD
    for j in range(16):
        for k in range(4):
            first = ge[2 * k, :, pl.ds((j // 2) * PAIR, PAIR)].astype(f32)
            second = ge[2 * k + 1, :, pl.ds((j // 2) * PAIR, PAIR)].astype(f32)
            if j % 2 == 0:
                second = pltpu.roll(second, HEAD, 1)
            else:
                first = pltpu.roll(first, HEAD, 1)
            update(2, (every, pl.ds(j * 512 + k * PAIR, PAIR)), jnp.where(left, first, second))

    flat[...] = jnp.zeros_like(flat)
    left = lax.broadcasted_iota(jnp.int32, (1, PAIR), 1) < HEAD

    def line(t, row):
        return vec[t // 4, t % 4, pl.ds(row, 1), :]

    for t in range(TPN):
        for i in range(2):
            for row, base in ((0, 0), (1, 16), (2, 80), (2, 160)):
                flat[pl.ds(base + 2 * t + i, 1), :] = line(t, 2 * row + i)
        for s in range(3):
            for hi in range(2):
                at = 32 + s * 16 + hi * 8 + t
                flat[pl.ds(at, 1), :] = line(t, 6 + 2 * s + 1 - hi)
    for j in range(16):
        for k in range(4):
            first = line(2 * k, 12 + j // 2)
            second = line(2 * k + 1, 12 + j // 2)
            if j % 2 == 0:
                second = pltpu.roll(second, HEAD, 1)
            else:
                first = pltpu.roll(first, HEAD, 1)
            flat[pl.ds(96 + 4 * j + k, 1), :] = jnp.where(left, first, second)
    z, y, c, x = (lax.axis_index(a) for a in ALL)
    number = ((z * 4 + y) * 2 + c) * 4 + x
    first = (176 * number) // 128
    own = jnp.concatenate([flat[pl.ds(first + i, 1), :] for i in range(3)], axis=1)
    own = jnp.broadcast_to(own, (8, 3 * PAIR))
    own = pltpu.roll(own, lax.rem(3 * PAIR - 16 * lax.rem(3 * number, 8), 3 * PAIR), 1)
    update(4, (every, every), own[0:1, 0:176])


def update_all(parts, masters, moments, seconds):
    f32 = jnp.float32
    vmem = pl.BlockSpec(memory_space=pltpu.VMEM)
    shapes = [jax.ShapeDtypeStruct(p.shape, p.dtype) for p in parts[:2]]
    for w in masters:
        shapes += [jax.ShapeDtypeStruct(w.shape, f32)] * 3
    return pl.pallas_call(
        update_kernel,
        in_specs=[vmem] * 22,
        out_specs=[vmem] * 17,
        out_shape=shapes,
        scratch_shapes=[pltpu.VMEM((184, PAIR), f32)],
        compiler_params=pltpu.CompilerParams(vmem_limit_bytes=62 * 2**20),
        name="update",
    )(*parts, *masters, *moments, *seconds)


def adam_step(weight, moment, second, gradient, step_rate, step_decay):
    moment_new = BETA_ONE * moment + (1 - BETA_ONE) * gradient
    second_new = BETA_TWO * second + (1 - BETA_TWO) * gradient * gradient
    moment_hat = moment_new / (1 - BETA_ONE**STEP)
    second_hat = second_new / (1 - BETA_TWO**STEP)
    updated = weight - step_rate * (
        moment_hat / (jnp.sqrt(second_hat) + ADAM_EPS) + step_decay * weight
    )
    return (second_new, updated)


def shards(
    tokens, cotangent, block_seq, seq_lengths,
    qkv_weight, qkv_moment, qkv_second,
    dense_weight, dense_moment, dense_second,
    expand_weight, expand_moment, expand_second,
    shrink_weight, shrink_moment, shrink_second,
    vectors, vec_moment, vec_second,
):
    parts = layer(
        tokens,
        cotangent,
        block_seq,
        seq_lengths,
        vectors,
        (qkv_weight, dense_weight, expand_weight, shrink_weight),
    )
    masters = (qkv_weight, dense_weight, expand_weight, shrink_weight, vectors[None, :])
    moments = (qkv_moment, dense_moment, expand_moment, shrink_moment, vec_moment[None, :])
    seconds = (qkv_second, dense_second, expand_second, shrink_second, vec_second[None, :])
    results = update_all(parts, masters, moments, seconds)
    return (*results[:14], *(r[0] for r in results[14:]))


def solution(mesh):
    finer = Mesh(mesh.devices.reshape(*SIZES), ALL)
    whole, group = P(ALL, None), P(DP, None)
    return jax.shard_map(
        shards,
        mesh=finer,
        in_specs=(whole, whole, group, group, *[whole] * 12, *[P(ALL)] * 3),
        out_specs=(*[whole] * 14, *[P(ALL)] * 3),
        check_vma=False,
    )
```

profile of v0, /device:TPU:1, one launch (start us, length us, event | category | flops | bytes accessed | tf_op | source)
XLA Modules:
  0.0 180.9 jit_solution(5672385408360428339)
XLA Ops:
  0.7 173.8 %layer.1 = (bf16[128,2048]{1,0:T(8,128)(2,1)}, bf16[128,2048]{1,0:T(8,128)(2,1)}, bf16[8,16,1024]{2,1,0:T(8,128)(2,1)}, bf16[8,16,768]{2,1,0:T(8,128)(2,1)}, bf1...) custom-call(bf16[128,2048]{1,0:T(8,128)(2,1)} %tokens_ref.1, bf16[128,2048]{1,0:T(8,128)(2,1)} %cot_ref.1, ...), custom_call_target="tpu_custom_call" | custom-call | tf_op jit(solution)/shard_map/layer/pallas_call | solution.py:1010
  174.4 6.2 %update.1 = (bf16[128,2048]{1,0:T(8,128)(2,1)}, bf16[128,2048]{1,0:T(8,128)(2,1)}, f32[16,6144]{1,0:T(8,128)}, f32[16,6144]{1,0:T(8,128)}, f32[16,6144]{1,0:T(8,...) custom-call(bf16[128,2048]{1,0:T(8,128)(2,1)} %get-tuple-element.41., ...), custom_call_target="tpu_custom_call" | custom-call | tf_op jit(solution)/shard_map/update/pallas_call | solution.py:1111
where the time goes:
time: 184 us; the launch traced here: 181 us
  Pallas kernels  180 us (98%)
    pallas_call x1, Pallas kernels, layer(): pl.pallas_call(layer_kernel, in_specs=[vmem, vmem, smem, smem, vmem, vmem...  174 us
    pallas_call x1, Pallas kernels, update_all(): pl.pallas_call(update_kernel, in_specs=[vmem] * 22, out_specs=[vmem] * 17...  6.23 us

commit v1 on v0

--- a/solution.py
+++ b/solution.py
@@ -25,16 +25,16 @@
 TPN = 8
 COPIES = 480
 SCHEDULE = (
-    "s", "vec", "to_d", "to_q", "d", "tok", "to_e", "q", "s", "cot", "vec_rows", "q", "tok",
-    "q", "e", "q", "norm_own", "cot", "norm_sides", "q", "norm_far", "e", "d_att", "qkv0", "e",
-    "qkv1", "s", "att0", "att1", "s", "e", "att2", "att3", "e", "s", "grad_q0", "grad_q1",
-    "sum_q", "grad_d", "up0", "up1", "up2", "sum_q", "up3", "grad_e0", "sum_e0", "sum_q",
-    "grad_e1", "downa1", "n1", "downb1", "sum_d", "sum_q", "sum_e1", "downa0", "n1", "downb0",
-    "n0", "grad_s0", "back_q", "sum_e0", "sum_d", "n0", "sum_e1", "grad_s1", "outa0", "n1",
-    "sum_d", "sum_s1", "sum_s0", "outa1", "col_sums", "sum_e1", "sum_d", "n0", "o1", "outb1",
-    "norm_back", "vec_back", "back_d", "o1", "o0", "sum_e0", "outb0", "sum_s1", "o0", "sum_e1",
-    "sum_s0", "back_e", "vec_back", "sum_s1", "sum_s0", "o0", "o1", "sum_s1", "sum_s0",
-    "vec_back", "sum_s1",
+    "to_q", "s", "to_d", "tok", "vec", "d", "q", "to_e", "cot", "vec_rows", "q", "q", "e", "q",
+    "norm_own", "q", "cot", "s", "norm_sides", "e", "norm_far", "qkv0", "d_att", "qkv1", "s",
+    "e", "att0", "att1", "s", "att2", "att3", "e", "grad_q0", "e", "s", "grad_q1", "grad_d",
+    "sum_d", "sum_q", "up0", "up1", "sum_d", "up2", "up3", "sum_q", "grad_e0", "grad_e1",
+    "sum_e1", "downa1", "downa0", "n1", "sum_q", "sum_e0", "downb1", "n1", "n0", "grad_s0",
+    "sum_q", "downb0", "sum_e1", "n0", "n1", "sum_e0", "grad_s1", "sum_d", "sum_s1", "outa1",
+    "outb1", "n0", "sum_s0", "o1", "sum_d", "col_sums", "back_q", "outa0", "sum_s1", "o1",
+    "norm_back", "back_d", "o0", "sum_e0", "outb0", "back_d", "vec_back", "sum_s0", "o0",
+    "sum_s1", "sum_e1", "sum_s0", "o1", "sum_e1", "vec_back", "o0", "back_e", "sum_s0",
+    "sum_s1", "vec_back", "sum_s1",
 )
 SCALE = HEAD ** (-0.5)
 

time: 184 us -> 194 us (1.054)
  Pallas kernels: 180 us -> 190 us
    pallas_call x1, Pallas kernels: 174 us -> 183 us  [layer(): pl.pallas_call(layer_kernel, in_specs=[vmem, vmem, smem, smem, vmem, vmem...]
where the time goes in v1:
time: 194 us; the launch traced here: 191 us
  Pallas kernels  190 us (98%)
    pallas_call x1, Pallas kernels, layer(): pl.pallas_call(layer_kernel, in_specs=[vmem, vmem, smem, smem, vmem, vmem...  183 us
    pallas_call x1, Pallas kernels, update_all(): pl.pallas_call(update_kernel, in_specs=[vmem] * 22, out_specs=[vmem] * 17...  6.23 us

profile of v1, /device:TPU:1, one launch (start us, length us, event | category | flops | bytes accessed | tf_op | source)
XLA Modules:
  0.0 190.5 jit_solution(12434861470550984826)
XLA Ops:
  0.7 183.4 %layer.1 = (bf16[128,2048]{1,0:T(8,128)(2,1)}, bf16[128,2048]{1,0:T(8,128)(2,1)}, bf16[8,16,1024]{2,1,0:T(8,128)(2,1)}, bf16[8,16,768]{2,1,0:T(8,128)(2,1)}, bf1...) custom-call(bf16[128,2048]{1,0:T(8,128)(2,1)} %tokens_ref.1, bf16[128,2048]{1,0:T(8,128)(2,1)} %cot_ref.1, ...), custom_call_target="tpu_custom_call" | custom-call | tf_op jit(solution)/shard_map/layer/pallas_call | solution.py:1010
  184.0 6.2 %update.1 = (bf16[128,2048]{1,0:T(8,128)(2,1)}, bf16[128,2048]{1,0:T(8,128)(2,1)}, f32[16,6144]{1,0:T(8,128)}, f32[16,6144]{1,0:T(8,128)}, f32[16,6144]{1,0:T(8,...) custom-call(bf16[128,2048]{1,0:T(8,128)(2,1)} %get-tuple-element.41., ...), custom_call_target="tpu_custom_call" | custom-call | tf_op jit(solution)/shard_map/update/pallas_call | solution.py:1111

commit v2 on v0

--- a/solution.py
+++ b/solution.py
@@ -25,15 +25,15 @@
 TPN = 8
 COPIES = 480
 SCHEDULE = (
-    "s", "vec", "to_d", "to_q", "d", "tok", "to_e", "q", "s", "cot", "vec_rows", "q", "tok",
-    "q", "e", "q", "norm_own", "cot", "norm_sides", "q", "norm_far", "e", "d_att", "qkv0", "e",
-    "qkv1", "s", "att0", "att1", "s", "e", "att2", "att3", "e", "s", "grad_q0", "grad_q1",
-    "sum_q", "grad_d", "up0", "up1", "up2", "sum_q", "up3", "grad_e0", "sum_e0", "sum_q",
-    "grad_e1", "downa1", "n1", "downb1", "sum_d", "sum_q", "sum_e1", "downa0", "n1", "downb0",
-    "n0", "grad_s0", "back_q", "sum_e0", "sum_d", "n0", "sum_e1", "grad_s1", "outa0", "n1",
-    "sum_d", "sum_s1", "sum_s0", "outa1", "col_sums", "sum_e1", "sum_d", "n0", "o1", "outb1",
-    "norm_back", "vec_back", "back_d", "o1", "o0", "sum_e0", "outb0", "sum_s1", "o0", "sum_e1",
-    "sum_s0", "back_e", "vec_back", "sum_s1", "sum_s0", "o0", "o1", "sum_s1", "sum_s0",
+    "vec", "to_q", "s", "to_d", "d", "tok", "q", "s", "to_e", "cot", "vec_rows", "q", "e",
+    "norm_own", "cot", "q", "norm_sides", "q", "norm_far", "q", "cot", "e", "d_att", "s",
+    "qkv0", "e", "qkv1", "att0", "att1", "s", "att2", "e", "att3", "e", "s", "grad_q0",
+    "grad_q1", "sum_q", "grad_d", "up0", "up1", "sum_d", "up2", "sum_q", "up3", "grad_e0",
+    "sum_d", "grad_e1", "sum_e1", "downa1", "n1", "sum_q", "downa0", "n0", "sum_d", "sum_e0",
+    "downb1", "n1", "downb0", "n0", "sum_q", "sum_e1", "grad_s0", "sum_d", "grad_s1", "sum_e0",
+    "back_q", "outa1", "n1", "col_sums", "sum_s0", "sum_e1", "outb1", "back_d", "n0", "sum_e0",
+    "sum_s1", "o1", "outa0", "sum_e1", "norm_back", "o1", "o0", "back_e", "sum_s1", "sum_s0",
+    "vec_back", "outb0", "o0", "vec_back", "sum_s1", "o1", "sum_s0", "o0", "sum_s1", "sum_s0",
     "vec_back", "sum_s1",
 )
 SCALE = HEAD ** (-0.5)

time: 184 us -> 181 us (0.984)
  Pallas kernels: 180 us -> 178 us
where the time goes in v2:
time: 181 us; the launch traced here: 179 us
  Pallas kernels  178 us (98%)
    pallas_call x1, Pallas kernels, layer(): pl.pallas_call(layer_kernel, in_specs=[vmem, vmem, smem, smem, vmem, vmem...  172 us
    pallas_call x1, Pallas kernels, update_all(): pl.pallas_call(update_kernel, in_specs=[vmem] * 22, out_specs=[vmem] * 17...  6.23 us

profile of v2, /device:TPU:1, one launch (start us, length us, event | category | flops | bytes accessed | tf_op | source)
XLA Modules:
  0.0 179.0 jit_solution(2775495819390286548)
XLA Ops:
  0.7 171.9 %layer.1 = (bf16[128,2048]{1,0:T(8,128)(2,1)}, bf16[128,2048]{1,0:T(8,128)(2,1)}, bf16[8,16,1024]{2,1,0:T(8,128)(2,1)}, bf16[8,16,768]{2,1,0:T(8,128)(2,1)}, bf1...) custom-call(bf16[128,2048]{1,0:T(8,128)(2,1)} %tokens_ref.1, bf16[128,2048]{1,0:T(8,128)(2,1)} %cot_ref.1, ...), custom_call_target="tpu_custom_call" | custom-call | tf_op jit(solution)/shard_map/layer/pallas_call | solution.py:1010
  172.6 6.2 %update.1 = (bf16[128,2048]{1,0:T(8,128)(2,1)}, bf16[128,2048]{1,0:T(8,128)(2,1)}, f32[16,6144]{1,0:T(8,128)}, f32[16,6144]{1,0:T(8,128)}, f32[16,6144]{1,0:T(8,...) custom-call(bf16[128,2048]{1,0:T(8,128)(2,1)} %get-tuple-element.41., ...), custom_call_target="tpu_custom_call" | custom-call | tf_op jit(solution)/shard_map/update/pallas_call | solution.py:1111
